TPU v7x, 32 devices: a whole 2x2x4 slice. The times are simulated.
32 devices in a mesh: groups: 2 (over y), fsdp: 4 (over z), mp: 2 (over x), sub: 2 (over core).
Axes of the slice: x: 2, y: 2, z: 4, core: 2. Of those that a mesh axis runs over, the one named last changes fastest.
Arguments:
- queries: bfloat16 [4096, 16384], P(('groups', 'fsdp', 'sub'), 'mp'), parts along dimension 0, may hold values from -68 to 68
- lengths: int32 [8], P('groups'), parts along dimension 0, may hold values from 1 to 512, 1024 in all
- prompt_x: bfloat16 [4096, 16384], P(('groups', 'fsdp', 'sub'), 'mp'), parts along dimension 0, may hold values from -6 to 6
- norm_gain: float32 [16384], replicated, may hold values from 0.1 to 1.9
- key_weight: bfloat16 [16384, 1024], P(('fsdp', 'sub'), 'mp'), may hold values from -0.046875 to 0.046875
- value_weight: bfloat16 [16384, 1024], P(('fsdp', 'sub'), 'mp'), may hold values from -0.046875 to 0.046875
Outputs:
- prefix_out: bfloat16 [4096, 16384], P(('groups', 'fsdp', 'sub'), 'mp'), parts along dimension 0
- prefix_lse: float32 [4096, 128], P(('groups', 'fsdp', 'sub'), 'mp'), parts along dimension 0
There are 2 independent parts, one for each index of `groups`. A program takes and returns all parts, laid end to end along the dimension named above; an argument that names none is the same for every part. Nothing has to cross between parts.
Inputs may be any that keep to these rules, and one draw needn't show every extreme that they name: The 4 lengths of a part sum to exactly 1024, and the largest is 512.
All inputs are finite; a program needn't handle non-finite values.
Results may differ from a plain program's by a relative error of at most 0.009.
The roundings to bfloat16 on the way count: a program that leaves them out, or rounds other values in their place, can miss the bound.
Values may be sent and summed in bfloat16 or wider, within the bound.
A program may use at most 128 MiB of HBM per device.

v0:
```python
import jax
import jax.numpy as jnp
from jax import lax
from jax.sharding import PartitionSpec as P

HD = 128
COMPL = 4


rope_base = 500000.0
norm_eps = 1e-05


def rotate(field, positions):
    half = field.shape[-1] // 2
    exponents = jnp.arange(half, dtype=jnp.float32) * (2.0 / field.shape[-1])
    freqs = jnp.exp(-exponents * jnp.log(jnp.float32(rope_base)))
    angles = positions.astype(jnp.float32)[:, None] * freqs[None, :]
    cosine = jnp.cos(angles)[:, None, :]
    sine = jnp.sin(angles)[:, None, :]
    first = field[..., :half]
    second = field[..., half:]
    return jnp.concatenate(
        [first * cosine - second * sine, second * cosine + first * sine], axis=-1
    )


def length_of(owner, lengths):
    table = jnp.arange(lengths.shape[0], dtype=jnp.int32)
    return jnp.sum(jnp.where(owner[:, None] == table[None, :], lengths[None, :], 0), axis=1)


def attend_rows(query_rows, all_keys, all_values, kv_heads):
    count_rows = query_rows.shape[0]
    head_width = HD
    group = query_rows.shape[1] // (kv_heads * head_width)
    outputs = []
    totals = []
    for head in range(kv_heads):
        q_part = query_rows[:, head * group * head_width : (head + 1) * group * head_width]
        q_part = q_part.reshape(count_rows, group, head_width)
        k_part = all_keys[:, head * head_width : (head + 1) * head_width]
        v_part = all_values[:, head * head_width : (head + 1) * head_width]
        scores = jnp.einsum(
            "rgd,pd->rgp", q_part, k_part, preferred_element_type=jnp.float32
        ) * head_width ** (-0.5)
        peak = jnp.max(scores, axis=-1, keepdims=True)
        expd = jnp.exp(scores - peak)
        total = jnp.sum(expd, axis=-1, keepdims=True)
        weights = (expd / total).astype(jnp.bfloat16)
        mixed = jnp.einsum("rgp,pd->rgd", weights, v_part, preferred_element_type=jnp.float32)
        outputs.append(mixed.reshape(count_rows, group * head_width))
        totals.append(peak[..., 0] + jnp.log(total[..., 0]))
    return (jnp.concatenate(outputs, axis=1).astype(jnp.bfloat16), jnp.concatenate(totals, axis=1))


def attend(query_rows, all_keys, all_values, kv_heads):
    count_rows = query_rows.shape[0]
    piece_rows = 32
    pieces = query_rows.reshape(count_rows // piece_rows, piece_rows, query_rows.shape[1])

    def one_piece(piece):
        return attend_rows(piece, all_keys, all_values, kv_heads)

    mixed, log_totals = lax.map(one_piece, pieces)
    return (
        mixed.reshape(count_rows, mixed.shape[2]),
        log_totals.reshape(count_rows, log_totals.shape[2]),
    )


def body(queries, lengths, prompt_x, norm_gain, key_weight, value_weight):
    group_size = lax.axis_size(("fsdp", "sub"))
    my_index = lax.axis_index(("fsdp", "sub"))
    prompt_rows = prompt_x.shape[0]
    kv_width = key_weight.shape[1]
    kv_heads = kv_width // HD
    full_rows = lax.all_gather(prompt_x, "mp", axis=1, tiled=True)
    widened = full_rows.astype(jnp.float32)
    mean_square = jnp.mean(widened * widened, axis=1, keepdims=True)
    normed = (widened * lax.rsqrt(mean_square + norm_eps) * norm_gain[None, :]).astype(jnp.bfloat16)
    slices = lax.all_to_all(normed, ("fsdp", "sub"), split_axis=1, concat_axis=0, tiled=True)
    joined_weights = jnp.concatenate([key_weight, value_weight], axis=1)
    summed = lax.psum_scatter(
        jnp.dot(slices, joined_weights, preferred_element_type=jnp.float32),
        ("fsdp", "sub"),
        scatter_dimension=0,
        tiled=True,
    )
    raw_keys = summed[:, :kv_width]
    raw_values = summed[:, kv_width:]
    positions = my_index * prompt_rows + jnp.arange(prompt_rows, dtype=jnp.int32)
    cache_keys = (
        rotate(raw_keys.reshape(prompt_rows, kv_heads, HD), positions)
        .reshape(prompt_rows, kv_width)
        .astype(jnp.bfloat16)
    )
    cache_values = raw_values.astype(jnp.bfloat16)
    all_keys, all_values = (
        lax.all_gather(cache_keys, ("fsdp", "sub"), axis=0, tiled=True),
        lax.all_gather(cache_values, ("fsdp", "sub"), axis=0, tiled=True),
    )
    rows_here = queries.shape[0]
    most_rows = rows_here * group_size // COMPL
    mixed, log_total = attend(queries, all_keys, all_values, kv_heads)
    row_ids = my_index * rows_here + jnp.arange(rows_here, dtype=jnp.int32)
    row_live = row_ids % most_rows < length_of(row_ids // most_rows, lengths)
    prefix_out = jnp.where(row_live[:, None], mixed, jnp.zeros_like(mixed))
    prefix_lse = jnp.where(row_live[:, None], log_total, jnp.zeros_like(log_total))
    return (prefix_out, prefix_lse)


def solution(mesh):
    return jax.shard_map(
        body,
        mesh=mesh,
        in_specs=(
            P(("groups", "fsdp", "sub"), "mp"),
            P("groups"),
            P(("groups", "fsdp", "sub"), "mp"),
            P(),
            P(("fsdp", "sub"), "mp"),
            P(("fsdp", "sub"), "mp"),
        ),
        out_specs=(P(("groups", "fsdp", "sub"), "mp"), P(("groups", "fsdp", "sub"), "mp")),
        check_vma=False,
    )
```

profile of v0, /device:TPU:0, one launch (start us, length us, event | category | flops | bytes accessed | tf_op | source)
XLA Modules:
  0.0 654.9 jit_solution(13158245045441038404)
XLA Ops:
  7.2 6.4 copy.13
  13.7 106.8 %all-gather.4.cloned.1.call-done = bf16[256,16384]{0,1:T(8,128)(2,1)} async-done(((bf16[256,8192]{0,1:T(8,128)(2,1)}), bf16[256,16384]{0,1:T(8,128)(2,1)}) %all-gather.4.cloned.1.call-update) | async-done | bytes 8388624 | tf_op jit(solution)/shard_map/all_gather | solution.py:78
  120.5 7.0 %fusion.37 = f32[256]{0:T(256)S(1)} fusion(bf16[256,16384]{0,1:T(8,128)(2,1)} %all-gather.4.cloned.1.call-done), kind=kLoop, calls=%fused_computation.62 | loop fusion | flops 12582656 | bytes 8389632 | tf_op jit(solution)/shard_map/reduce_sum | solution.py:80
  127.5 6.9 %fusion.39 = bf16[256,16384]{0,1:T(8,128)(2,1)S(1)} fusion(bf16[256,16384]{0,1:T(8,128)(2,1)S(1)} %copy-done.1, f32[16384]{0:T(1024)S(1)} %copy-done.2, f32[256]{0:T(256)S(1)} %add_rsqrt_fusion), kind=kLoop, calls=%fused_computation.64 | loop fusion | flops 16777216 | bytes 16843776 | tf_op jit(solution)/shard_map/convert_element_type | solution.py:81
  134.4 188.6 %all_to_all.19 = bf16[256,8,2048]{0,2,1:T(8,128)(2,1)} all-to-all(bf16[256,8,2048]{0,2,1:T(8,128)(2,1)S(1)} %bitcast.105), channel_id=1, replica_groups=mesh['groups'=2,'fsdp'=4,'mp'=2,'sub'=2] {'fsdp','sub'}, dimensions={1} | all-to-all | bytes 16777216 | tf_op jit(solution)/shard_map/all_to_all | solution.py:82
  323.0 11.7 %copy.14 = bf16[8,256,2048]{2,1,0:T(8,128)(2,1)} copy(bf16[8,256,2048]{1,2,0:T(8,128)(2,1)} %bitcast.106) | data formatting | bytes 16777216 | tf_op jit(solution)/shard_map/all_to_all | solution.py:82
  334.7 13.8 %fusion.40 = f32[2048,1024]{1,0:T(8,128)} fusion(bf16[2048,2048]{1,0:T(8,128)(2,1)} %bitcast.111, bf16[2048,512]{1,0:T(8,128)(2,1)S(1)} %copy-done.5, bf16[2048,512]{1,0:T(8,128)(2,1)} %param.12), kind=kOutput, calls=%fused_computation.65 | convolution fusion | flops 8598323200 | bytes 20971520 | tf_op jit(solution)/shard_map/dot_general | solution.py:85
  349.2 86.8 %reduce-scatter.2.cloned.1.call-done = f32[256,1024]{1,0:T(8,128)} async-done(((f32[2048,1024]{1,0:T(8,128)}), f32[256,1024]{1,0:T(8,128)}) %reduce-scatter.2.cloned.1.call-update) | async-done | bytes 1048592 | tf_op jit(solution)/shard_map/reduce_scatter | solution.py:84
  441.6 24.9 %all-gather.6.cloned.1.call-done = bf16[2048,512]{1,0:T(8,128)(2,1)} async-done(((bf16[256,512]{1,0:T(8,128)(2,1)}), bf16[2048,512]{1,0:T(8,128)(2,1)}) %all-gather.6.cloned.1.call-update) | async-done | bytes 2097168 | tf_op jit(solution)/shard_map/all_gather | solution.py:100
  466.5 30.1 %all-gather.8.cloned.1.call-done = bf16[2048,512]{1,0:T(8,128)(2,1)} async-done(((bf16[256,512]{1,0:T(8,128)(2,1)}), bf16[2048,512]{1,0:T(8,128)(2,1)}) %all-gather.8.cloned.1.call-update) | async-done | bytes 2097168 | tf_op jit(solution)/shard_map/all_gather | solution.py:101
  496.6 146.3 %while.12 = (s32[]{:T(128)}, bf16[8,32,8192]{2,1,0:T(8,128)(2,1)}, f32[8,32,64]{2,1,0:T(8,128)S(1)}, bf16[8,32,8192]{2,1,0:T(8,128)(2,1)}, bf16[2048,512]{1,0:T(...) while((s32[]{:T(128)}, bf16[8,32,8192]{2,1,0:T(8,128)(2,1)}, f32[8,32,64]{2,1,0:T(8,128)S(1)}, ...), condition=%wide.region_12.13_spmd, body=%wide.region_3.12_spmd.sunk | while | flops 2187595776 | bytes 69353584 | solution.py:65
  497.9 1.8 multiply_reduce_fusion.11
  500.5 2.2 fusion.85
  504.4 2.1 fusion.83
  508.1 2.1 fusion.81
  511.8 2.1 fusion.79
  516.1 1.8 multiply_reduce_fusion.11
  518.8 2.2 fusion.85
  522.6 2.1 fusion.83
  526.4 2.1 fusion.81
  530.1 2.1 fusion.79
  537.1 2.2 fusion.85
  540.9 2.1 fusion.83
  544.7 2.1 fusion.81
  548.4 2.1 fusion.79
  552.7 1.8 multiply_reduce_fusion.11
  555.4 2.2 fusion.85
  559.3 2.1 fusion.83
  563.0 2.1 fusion.81
  566.7 2.1 fusion.79
  573.7 2.2 fusion.85
  577.5 2.1 fusion.83
  581.3 2.1 fusion.81
  585.0 2.1 fusion.79
  589.3 1.8 multiply_reduce_fusion.11
  592.0 2.2 fusion.85
  595.8 2.1 fusion.83
  599.6 2.1 fusion.81
  603.3 2.1 fusion.79
  610.3 2.2 fusion.85
  614.1 2.1 fusion.83
  617.9 2.1 fusion.81
  621.6 2.1 fusion.79
  628.5 2.2 fusion.85
  632.4 2.1 fusion.83
  636.2 2.1 fusion.81
  639.9 2.1 fusion.79
  643.8 4.5 bitcast_select_fusion
  (222 shorter events, 77.6 us)
Async XLA Ops:
  7.2 113.3 %all-gather.4.cloned.1.call-start = ((), (), s32[]{:S(2)}) async-start(), calls=%async_computation.2 | async-start | bytes 12582912 | tf_op jit(solution)/shard_map/all_gather | solution.py:78
  13.6 113.9 %copy-start.2 = (f32[16384]{0:T(1024)S(1)}, f32[16384]{0:T(1024)}, u32[]{:S(2)}) copy-start(f32[16384]{0:T(1024)} %param.11) | copy-start | bytes 196612
  13.6 422.4 %reduce-scatter.2.cloned.1.call-start = ((), (), s32[]{:S(2)}) async-start(), calls=%async_computation.3 | async-start | bytes 9437184 | tf_op jit(solution)/shard_map/reduce_scatter | solution.py:84
  120.5 7.1 %copy-start.1 = (bf16[256,16384]{0,1:T(8,128)(2,1)S(1)}, bf16[256,16384]{0,1:T(8,128)(2,1)}, u32[]{:S(2)}) copy-start(bf16[256,16384]{0,1:T(8,128)(2,1)} %all-gather.4.cloned.1.call-done) | copy-start | bytes 25165828
  323.0 11.7 %copy-start.5 = (bf16[2048,512]{1,0:T(8,128)(2,1)S(1)}, bf16[2048,512]{1,0:T(8,128)(2,1)}, u32[]{:S(2)}) copy-start(bf16[2048,512]{1,0:T(8,128)(2,1)} %param.13) | copy-start | bytes 6291460
  348.6 92.4 %copy-start.4 = (s32[4]{0:T(128)S(1)}, s32[4]{0:T(128)}, u32[]{:S(2)}) copy-start(s32[4]{0:T(128)} %param.9) | copy-start | bytes 52
  348.6 118.0 %all-gather.6.cloned.1.call-start = ((), (), s32[]{:S(2)}) async-start(), calls=%async_computation.4 | async-start | bytes 2359296 | tf_op jit(solution)/shard_map/all_gather | solution.py:100
  438.9 57.7 %all-gather.8.cloned.1.call-start = ((), (), s32[]{:S(2)}) async-start(), calls=%async_computation.5 | async-start | bytes 2359296 | tf_op jit(solution)/shard_map/all_gather | solution.py:101
  496.6 146.4 %copy-start.3 = (pred[256]{0:T(512)(128)(4,1)S(1)}, pred[256]{0:T(512)(128)(4,1)}, u32[]{:S(2)}) copy-start(pred[256]{0:T(512)(128)(4,1)} %fusion.44) | copy-start | bytes 772
  500.5 2.3 copy-start
  518.8 2.3 copy-start
  537.1 2.3 copy-start
  555.4 2.3 copy-start
  573.7 2.3 copy-start
  592.0 2.3 copy-start
  610.3 2.3 copy-start
  628.5 2.3 copy-start
Sparse Core Ops, SparseCore 0:
  13.7 106.6 all-gather.3
  348.7 87.2 reduce-scatter.1
  439.0 27.4 all-gather.5
  468.0 28.5 all-gather.7
where the time goes:
time: 658 us; the launch traced here: 655 us
  waiting for transfers between devices  249 us (38%)
  blocking collectives  189 us (29%)
  matrix products  114 us (17%)
  other arithmetic  53.5 us (8%)
  local copies, waits for them, and re-layouts  34.1 us (5%)
  between operations  13.9 us (2%)
    all_to_all x1, blocking collectives, body(): lax.all_to_all(normed, ('fsdp', 'sub'), split_axis=1, concat_axis=0, tile...  189 us
    all_gather x1, waiting for transfers between devices, body(): full_rows = lax.all_gather(prompt_x, 'mp', axis=1, tiled=True)  107 us
    reduce_scatter x1, waiting for transfers between devices, body(): lax.psum_scatter(jnp.dot(slices, joined_weights, preferred_element_type=j...  86.8 us
    dot_general x32, matrix products, attend_rows(): jnp.einsum('rgp,pd->rgd', weights, v_part, preferred_element_type=jnp.flo...  67.4 us
    dot_general x32, matrix products, attend_rows(): jnp.einsum('rgd,pd->rgp', q_part, k_part, preferred_element_type=jnp.floa...  33.3 us
    all_gather x1, waiting for transfers between devices, body(): lax.all_gather(cache_values, ('fsdp', 'sub'), axis=0, tiled=True)  30.1 us
    reduce_sum x32, other arithmetic, attend_rows(): total = jnp.sum(expd, axis=-1, keepdims=True)  25.3 us
    all_gather x1, waiting for transfers between devices, body(): lax.all_gather(cache_keys, ('fsdp', 'sub'), axis=0, tiled=True)  24.9 us
  transfers between devices with their start and end apart: 4, of which 4 were waited for; matrix products, arithmetic and copies ran while one was open for 0% of the time, Pallas kernels for 0%

commit v1 on v0

v1 whole, which is shorter than its diff:
```python
import functools

import jax
import jax.numpy as jnp
from jax import lax
from jax.experimental import pallas as pl
from jax.experimental.pallas import tpu as pltpu
from jax.sharding import PartitionSpec as P

MESH = pl.DeviceIdType.MESH

HD = 128
COMPL = 4


rope_base = 500000.0
norm_eps = 1e-05


def rotate(field, positions):
    half = field.shape[-1] // 2
    exponents = jnp.arange(half, dtype=jnp.float32) * (2.0 / field.shape[-1])
    freqs = jnp.exp(-exponents * jnp.log(jnp.float32(rope_base)))
    angles = positions.astype(jnp.float32)[:, None] * freqs[None, :]
    cosine = jnp.cos(angles)[:, None, :]
    sine = jnp.sin(angles)[:, None, :]
    first = field[..., :half]
    second = field[..., half:]
    return jnp.concatenate(
        [first * cosine - second * sine, second * cosine + first * sine], axis=-1
    )


def length_of(owner, lengths):
    table = jnp.arange(lengths.shape[0], dtype=jnp.int32)
    return jnp.sum(jnp.where(owner[:, None] == table[None, :], lengths[None, :], 0), axis=1)


def attend_kernel(heads, group, live_ref, q_ref, k_ref, v_ref, out_ref, lse_ref):
    step = pl.program_id(0)
    coeff = HD ** (-0.5) * 1.4426950408889634
    live = live_ref[...] > 0.0
    lane = lax.broadcasted_iota(jnp.int32, lse_ref.shape, 1)
    lse = lse_ref[...]
    for h in range(heads):
        cols = slice(h * HD, (h + 1) * HD)
        scores = lax.dot_general(
            q_ref[:, cols], k_ref[...], (((1,), (1,)), ((), ())), preferred_element_type=jnp.float32
        )
        peak = jnp.max(scores, axis=1, keepdims=True)
        expd = jnp.exp2(scores * coeff - peak * coeff)
        total = jnp.sum(expd, axis=1, keepdims=True)
        mixed = jnp.dot(expd.astype(jnp.bfloat16), v_ref[...], preferred_element_type=jnp.float32)
        mixed = mixed / total
        out_ref[:, cols] = jnp.where(live, mixed, 0.0).astype(jnp.bfloat16)
        value = jnp.where(live, peak * HD ** (-0.5) + jnp.log(total), 0.0)
        lse = jnp.where(lane == step * heads + h, value, lse)
    lse_ref[...] = lse


def attend(query_rows, keys, values, row_live, kv_heads, k_base=0, v_base=0):
    rows, width = query_rows.shape
    prompt = keys.shape[0]
    q_heads = width // HD
    group = q_heads // kv_heads
    heads = 4
    live = row_live.astype(jnp.float32)[:, None]
    return pl.pallas_call(
        functools.partial(attend_kernel, heads, group),
        grid=(q_heads // heads,),
        out_shape=(
            jax.ShapeDtypeStruct((rows, width), jnp.bfloat16),
            jax.ShapeDtypeStruct((rows, q_heads), jnp.float32),
        ),
        in_specs=[
            pl.BlockSpec((rows, 1), lambda i: (0, 0)),
            pl.BlockSpec((rows, heads * HD), lambda i: (0, i)),
            pl.BlockSpec((prompt, HD), lambda i: (0, k_base + i * heads // group)),
            pl.BlockSpec((prompt, HD), lambda i: (0, v_base + i * heads // group)),
        ],
        out_specs=(
            pl.BlockSpec((rows, heads * HD), lambda i: (0, i)),
            pl.BlockSpec((rows, q_heads), lambda i: (0, 0)),
        ),
        compiler_params=pltpu.CompilerParams(vmem_limit_bytes=48 * 1024 * 1024),
    )(live, query_rows, keys, values)


def live_rows(lengths, my_index, rows_here, group_size):
    most_rows = rows_here * group_size // COMPL
    row_ids = my_index * rows_here + jnp.arange(rows_here, dtype=jnp.int32)
    return row_ids % most_rows < length_of(row_ids // most_rows, lengths)


def hello():
    groups, fsdp, mp, sub = (lax.axis_index(a) for a in ("groups", "fsdp", "mp", "sub"))
    depth = lax.axis_size("fsdp")
    barrier = pltpu.get_barrier_semaphore()
    count = 0
    for dz in range(depth):
        for dx in range(2):
            for dc in range(2):
                if (dz, dx, dc) == (0, 0, 0):
                    continue
                target = (groups, lax.rem(fsdp + dz, depth), lax.rem(mp + dx, 2), lax.rem(sub + dc, 2))
                pl.semaphore_signal(barrier, inc=1, device_id=target, device_id_type=MESH)
                count += 1
    pl.semaphore_signal(barrier, inc=1, device_id=(1 - groups, fsdp, mp, sub), device_id_type=MESH)
    pl.semaphore_wait(barrier, count + 1)


def move_kernel(
    x_ref, kw_ref, vw_ref, xin, kwo, vwo, relay,
    relay_send, relay_recv, x_send, x_recv, x_local, w_send, w_recv, f_send, f_recv,
):
    groups, fsdp, mp, sub = (lax.axis_index(a) for a in ("groups", "fsdp", "mp", "sub"))
    depth = lax.axis_size("fsdp")
    parts = 2 * depth // 2
    width = x_ref.shape[1] // parts
    hello()
    mine = sub == mp

    def relay_copy(j):
        return pltpu.make_async_remote_copy(
            src_ref=x_ref.at[:, pl.ds(j * width, width)],
            dst_ref=relay.at[j],
            send_sem=relay_send.at[j],
            recv_sem=relay_recv.at[j],
            device_id=(groups, fsdp, 1 - mp, 1 - sub),
            device_id_type=MESH,
        )

    def order(n):
        return parts - 1 - n

    half = kw_ref.shape[0] // 2
    near = pl.ds(pl.multiple_of(groups * half, half), half)

    def weight_copy(i, src, dst):
        return pltpu.make_async_remote_copy(
            src_ref=src.at[near, :], dst_ref=dst.at[near, :],
            send_sem=w_send.at[i], recv_sem=w_recv.at[i],
            device_id=(groups, fsdp, 1 - mp, sub), device_id_type=MESH,
        )

    def weight_forward(i, dst):
        return pltpu.make_async_remote_copy(
            src_ref=dst.at[near, :], dst_ref=dst.at[near, :],
            send_sem=f_send.at[i], recv_sem=f_recv.at[i],
            device_id=(1 - groups, fsdp, mp, sub), device_id_type=MESH,
        )

    def target(j):
        return (depth // 2) * sub + j // 2, j % 2

    def chunk_copy(j, src):
        tz, tc = target(j)
        return pltpu.make_async_remote_copy(
            src_ref=src, dst_ref=xin.at[fsdp], send_sem=x_send.at[j], recv_sem=x_recv.at[fsdp],
            device_id=(groups, tz, mp, tc), device_id_type=MESH,
        )

    def send_chunk(j, src):
        tz, tc = target(j)
        here = jnp.logical_and(tz == fsdp, tc == sub)

        @pl.when(here)
        def _():
            pltpu.make_async_copy(src, xin.at[fsdp], x_local).start()

        @pl.when(jnp.logical_not(here))
        def _():
            chunk_copy(j, src).start()

    def finish_chunk(j, src):
        tz, tc = target(j)
        here = jnp.logical_and(tz == fsdp, tc == sub)

        @pl.when(here)
        def _():
            pltpu.make_async_copy(src, xin.at[fsdp], x_local).wait()

        @pl.when(jnp.logical_not(here))
        def _():
            chunk_copy(j, src).wait_send()

    weights = ((kw_ref, kwo), (vw_ref, vwo))

    @pl.when(jnp.logical_not(mine))
    def _():
        for n in range(parts):
            relay_copy(order(n)).start()

    @pl.when(mine)
    def _():
        for n in range(parts):
            j = order(n)
            send_chunk(j, x_ref.at[:, pl.ds(j * width, width)])

    for i, (src, dst) in enumerate(weights):
        weight_copy(i, src, dst).start()

    @pl.when(jnp.logical_not(mine))
    def _():
        for n in range(parts):
            j = order(n)
            relay_copy(j).wait_recv()
            send_chunk(j, relay.at[j])

    for i, (src, dst) in enumerate(weights):
        weight_copy(i, src, dst).wait_recv()
        weight_forward(i, dst).start()

    @pl.when(mine)
    def _():
        for n in range(parts):
            j = order(n)
            finish_chunk(j, x_ref.at[:, pl.ds(j * width, width)])

    @pl.when(jnp.logical_not(mine))
    def _():
        for n in range(parts):
            j = order(n)
            relay_copy(j).wait_send()
            finish_chunk(j, relay.at[j])

    for z in range(depth):
        here = jnp.logical_and(fsdp == z, fsdp // (depth // 2) == sub)

        @pl.when(jnp.logical_not(here))
        def _():
            pltpu.make_async_remote_copy(
                src_ref=xin.at[z], dst_ref=xin.at[z], send_sem=x_send.at[0], recv_sem=x_recv.at[z],
                device_id=(groups, z, mp, fsdp // (depth // 2)), device_id_type=MESH,
            ).wait_recv()

    far = pl.ds(pl.multiple_of((1 - groups) * half, half), half)
    for i, (src, dst) in enumerate(weights):
        weight_copy(i, src, dst).wait_send()
        weight_forward(i, dst).wait_send()
        pltpu.make_async_remote_copy(
            src_ref=dst.at[far, :], dst_ref=dst.at[far, :],
            send_sem=f_send.at[i], recv_sem=f_recv.at[i],
            device_id=(1 - groups, fsdp, mp, sub), device_id_type=MESH,
        ).wait_recv()


def move(prompt_x, key_weight, value_weight):
    depth = lax.axis_size("fsdp")
    rows = prompt_x.shape[0]
    width = key_weight.shape[0]
    parts = prompt_x.shape[1] // width
    anywhere = pl.BlockSpec(memory_space=pl.ANY)
    dma = pltpu.SemaphoreType.DMA
    return pl.pallas_call(
        move_kernel,
        out_shape=(
            jax.ShapeDtypeStruct((depth, rows, width), jnp.bfloat16),
            jax.ShapeDtypeStruct(key_weight.shape, jnp.bfloat16),
            jax.ShapeDtypeStruct(value_weight.shape, jnp.bfloat16),
            jax.ShapeDtypeStruct((parts, rows, width), jnp.bfloat16),
        ),
        in_specs=[anywhere] * 3,
        out_specs=(anywhere,) * 4,
        scratch_shapes=[
            dma((parts,)), dma((parts,)), dma((parts,)), dma((depth,)), dma(()),
            dma((2,)), dma((2,)), dma((2,)), dma((2,)),
        ],
        compiler_params=pltpu.CompilerParams(collective_id=0, has_side_effects=True),
    )(prompt_x, key_weight, value_weight)


def body_split(queries, lengths, prompt_x, norm_gain, key_weight, value_weight):
    depth = lax.axis_size("fsdp")
    fsdp, mp, sub = (lax.axis_index(a) for a in ("fsdp", "mp", "sub"))
    my_index = fsdp * 2 + sub
    prompt_rows = prompt_x.shape[0]
    features, kv_width = key_weight.shape
    kv_heads = kv_width // HD
    widened = prompt_x.astype(jnp.float32)
    squares = jnp.sum(widened * widened, axis=1)
    squares = lax.all_gather(squares, ("mp", "fsdp", "sub"), axis=0, tiled=False)
    squares = squares.reshape(2, depth, 2, prompt_rows).sum(axis=0)
    squares = lax.dynamic_index_in_dim(squares, mp, axis=1, keepdims=False).reshape(depth * prompt_rows)
    scale = lax.rsqrt(squares / norm_gain.shape[0] + norm_eps)
    gathered, other_key, other_value, _ = move(prompt_x, key_weight, value_weight)
    gain = lax.dynamic_slice_in_dim(norm_gain, my_index * features, features)
    gathered = gathered.reshape(depth * prompt_rows, features).astype(jnp.float32)
    normed = (gathered * scale[:, None] * gain[None, :]).astype(jnp.bfloat16)
    weights = jnp.concatenate([key_weight, value_weight, other_key, other_value], axis=1)
    summed = lax.psum_scatter(
        jnp.dot(normed, weights, preferred_element_type=jnp.float32),
        ("fsdp", "sub"), scatter_dimension=0, tiled=True,
    )
    rows = summed.shape[0]
    positions = (fsdp * 2 + mp) * prompt_rows + sub * rows + jnp.arange(rows, dtype=jnp.int32)
    own_keys, own_values, far_keys, far_values = (
        summed[:, i * kv_width : (i + 1) * kv_width] for i in range(4)
    )
    turn = lambda keys: rotate(keys.reshape(rows, kv_heads, HD), positions).reshape(rows, kv_width)
    near = jnp.concatenate([turn(own_keys), own_values], axis=1).astype(jnp.bfloat16)
    far = jnp.concatenate([turn(far_keys), far_values], axis=1).astype(jnp.bfloat16)
    arrived = lax.ppermute(far, "mp", [(0, 1), (1, 0)])
    both = jnp.concatenate([near, arrived], axis=0)
    cache = lax.all_gather(both, ("fsdp", "sub"), axis=0, tiled=True)
    live = live_rows(lengths, my_index, queries.shape[0], depth * 2)
    return attend(queries, cache, cache, live, kv_heads, 0, kv_heads)


def body(queries, lengths, prompt_x, norm_gain, key_weight, value_weight):
    group_size = lax.axis_size(("fsdp", "sub"))
    my_index = lax.axis_index(("fsdp", "sub"))
    prompt_rows = prompt_x.shape[0]
    kv_width = key_weight.shape[1]
    kv_heads = kv_width // HD
    full_rows = lax.all_gather(prompt_x, "mp", axis=1, tiled=True)
    widened = full_rows.astype(jnp.float32)
    mean_square = jnp.mean(widened * widened, axis=1, keepdims=True)
    normed = (widened * lax.rsqrt(mean_square + norm_eps) * norm_gain[None, :]).astype(jnp.bfloat16)
    slices = lax.all_to_all(normed, ("fsdp", "sub"), split_axis=1, concat_axis=0, tiled=True)
    joined_weights = jnp.concatenate([key_weight, value_weight], axis=1)
    summed = lax.psum_scatter(
        jnp.dot(slices, joined_weights, preferred_element_type=jnp.float32),
        ("fsdp", "sub"),
        scatter_dimension=0,
        tiled=True,
    )
    raw_keys = summed[:, :kv_width]
    raw_values = summed[:, kv_width:]
    positions = my_index * prompt_rows + jnp.arange(prompt_rows, dtype=jnp.int32)
    cache_keys = (
        rotate(raw_keys.reshape(prompt_rows, kv_heads, HD), positions)
        .reshape(prompt_rows, kv_width)
        .astype(jnp.bfloat16)
    )
    cache_values = raw_values.astype(jnp.bfloat16)
    all_keys, all_values = (
        lax.all_gather(cache_keys, ("fsdp", "sub"), axis=0, tiled=True),
        lax.all_gather(cache_values, ("fsdp", "sub"), axis=0, tiled=True),
    )
    live = live_rows(lengths, my_index, queries.shape[0], group_size)
    return attend(queries, all_keys, all_values, live, kv_heads)


def solution(mesh):
    sizes = mesh.shape
    split = sizes["mp"] == 2 and sizes["sub"] == 2 and sizes["groups"] == 2 and sizes["fsdp"] == 4
    return jax.shard_map(
        body_split if split else body,
        mesh=mesh,
        in_specs=(
            P(("groups", "fsdp", "sub"), "mp"),
            P("groups"),
            P(("groups", "fsdp", "sub"), "mp"),
            P(),
            P(("fsdp", "sub"), "mp"),
            P(("fsdp", "sub"), "mp"),
        ),
        out_specs=(P(("groups", "fsdp", "sub"), "mp"), P(("groups", "fsdp", "sub"), "mp")),
        check_vma=False,
    )
```

time: 658 us -> 396 us (0.60)
  Pallas kernels: 0 us -> 181 us
  blocking collectives: 189 us -> 23.1 us
  matrix products: 114 us -> 14.8 us
  waiting for transfers between devices: 249 us -> 150 us
  other arithmetic: 53.5 us -> 5.35 us
  local copies, waits for them, and re-layouts: 34.1 us -> 4.51 us
    all_to_all x1 -> x0, blocking collectives: 189 us -> none  [body(): lax.all_to_all(normed, ('fsdp', 'sub'), split_axis=1, concat_axis=0, tile...]
    pallas_call x0 -> x2, Pallas kernels: none -> 181 us  [the longest x1 118 us: move(): pl.pallas_call(move_kernel, out_shape=(jax.ShapeDtypeStruct((depth, rows,...]
    all_gather x3 -> x1, waiting for transfers between devices: 162 us -> 47 us  [body_split(): cache = lax.all_gather(both, ('fsdp', 'sub'), axis=0, tiled=True)]
    dot_general x65 -> x1, matrix products: 114 us -> 14.8 us  [body_split(): jnp.dot(normed, weights, preferred_element_type=jnp.float32)]
    reduce_sum x33 -> x2, other arithmetic: 32.4 us -> 3.12 us  [the longest x1 3.1 us: body_split(): squares = jnp.sum(widened * widened, axis=1)]
    all_gather x0 -> x1, blocking collectives: none -> 23.1 us  [body_split(): lax.all_gather(squares, ('mp', 'fsdp', 'sub'), axis=0, tiled=False)]
    reduce_scatter x1, waiting for transfers between devices: 86.8 us -> 98.6 us  [body_split(): lax.psum_scatter(jnp.dot(normed, weights, preferred_element_type=jnp.floa...]
    all_to_all x1 -> x0, local copies, waits for them, and re-layouts: 11.7 us -> none  [body(): lax.all_to_all(normed, ('fsdp', 'sub'), split_axis=1, concat_axis=0, tile...]
  transfers between devices with their start and end apart: 4 -> 3, of which waited for: 4 -> 3; matrix products, arithmetic and copies ran while one was open for 0% -> 0% of each run, Pallas kernels for 0% -> 0%
where the time goes in v1:
time: 396 us; the launch traced here: 395 us
  Pallas kernels  181 us (46%)
  waiting for transfers between devices  150 us (38%)
  blocking collectives  23.1 us (6%)
  matrix products  14.8 us (4%)
  between operations  14.3 us (4%)
  other arithmetic  5.35 us (1%)
  local copies, waits for them, and re-layouts  4.51 us (1%)
    pallas_call x1, Pallas kernels, move(): pl.pallas_call(move_kernel, out_shape=(jax.ShapeDtypeStruct((depth, rows,...  118 us
    reduce_scatter x1, waiting for transfers between devices, body_split(): lax.psum_scatter(jnp.dot(normed, weights, preferred_element_type=jnp.floa...  98.6 us
    pallas_call x1, Pallas kernels, attend(): pl.pallas_call(functools.partial(attend_kernel, heads, group), grid=(q_he...  62.7 us
    all_gather x1, waiting for transfers between devices, body_split(): cache = lax.all_gather(both, ('fsdp', 'sub'), axis=0, tiled=True)  47 us
    all_gather x1, blocking collectives, body_split(): lax.all_gather(squares, ('mp', 'fsdp', 'sub'), axis=0, tiled=False)  23.1 us
    dot_general x1, matrix products, body_split(): jnp.dot(normed, weights, preferred_element_type=jnp.float32)  14.8 us
  transfers between devices with their start and end apart: 3, of which 3 were waited for; matrix products, arithmetic and copies ran while one was open for 0% of the time, Pallas kernels for 0%

profile of v1, /device:TPU:0, one launch (start us, length us, event | category | flops | bytes accessed | tf_op | source)
XLA Modules:
  0.0 395.5 jit_solution(9169165492751898808)
XLA Ops:
  7.2 0.0 reduce-scatter.2.cloned.1.call-start
  7.2 3.1 multiply_reduce_fusion
  10.3 23.1 %all-gather.1 = f32[16,1,256]{2,1,0:T(1,128)S(1)} all-gather(f32[1,1,256]{2,1,0:T(1,128)S(1)} %bitcast.17), channel_id=2, replica_groups=mesh['groups'=2,'fsdp'=4,'mp'=2,'sub'=2] {'mp','fsdp','sub'}, dimensions={0}, use_global_device_ids=true | all-gather | bytes 17408 | tf_op jit(solution)/shard_map/all_gather | solution.py:282
  33.5 0.0 copy-start.2
  33.5 0.0 dynamic-slice-start
  33.6 118.5 %shard_map.77 = (bf16[4,256,2048]{2,1,0:T(8,128)(2,1)}, bf16[2048,512]{1,0:T(8,128)(2,1)}, bf16[2048,512]{1,0:T(8,128)(2,1)}, bf16[4,256,2048]{2,1,0:T(8,128)(2,1)}) custom-call(bf16[256,8192]{1,0:T(8,128)(2,1)} %x_ref.1, bf16[2048,512]{1,0:T(8,128)(2,1)} %kw_ref.1, bf16[2048,512]{1,0:T(8,128)(2,1)} %vw_ref.1), custom_call_target="tpu_custom_call" | custom-call | tf_op jit(solution)/shard_map/pallas_call | solution.py:255
  152.0 0.0 copy-done.2
  152.1 0.0 dynamic-slice-done
  152.1 14.8 %fusion = f32[1024,2048]{1,0:T(8,128)} fusion(bf16[2048,512]{1,0:T(8,128)(2,1)} %get-tuple-element.7, bf16[2048,512]{1,0:T(8,128)(2,1)} %get-tuple-element.6, bf16[2048,512]{1,0:T(8,128)(2,1)} %vw_ref.1, bf16[2048,512]{1,0:T(8,128)(2,1)S(1)} %copy-done.2, bf16[1024,2048]{1,0:T(8,128)(2,1)} %bitcast.20, f32[2048]{0:T(1024)S(1)} %dynamic-slice-done, ...), kind=kOutput, calls=%fused_computation | convolution fusion | flops 8631877632 | bytes 20983808 | tf_op jit(solution)/shard_map/dot_general | solution.py:292
  166.9 0.0 reduce-scatter.2.cloned.1.call-update
  166.9 0.2 all-gather.4.cloned.1.call-start
  167.2 0.3 multiply_cosine_fusion
  167.5 98.6 %reduce-scatter.2.cloned.1.call-done = f32[128,2048]{1,0:T(8,128)} async-done(((f32[1024,2048]{1,0:T(8,128)}), f32[128,2048]{1,0:T(8,128)}) %reduce-scatter.2.cloned.1.call-update) | async-done | bytes 1048592 | tf_op jit(solution)/shard_map/reduce_scatter | solution.py:291
  266.0 0.0 copy-start.1
  266.0 1.2 fusion.16
  267.2 0.0 copy-start.3
  267.2 0.1 reshape.167
  267.3 0.1 reshape.169
  267.4 0.4 subtract_convert_fusion.1
  267.9 0.4 pad_maximum_fusion.2
  268.2 0.0 copy-done.1
  268.3 0.1 convert.25
  268.4 1.5 collective-permute-start
  269.9 4.9 %collective-permute-done = bf16[128,1024]{1,0:T(8,128)(2,1)S(1)} collective-permute-done((bf16[128,1024]{1,0:T(8,128)(2,1)S(1)}, bf16[128,1024]{1,0:T(8,128)(2,1)S(1)}, u32[]{:S(2)}, u32[]{:S(2)}) %collective-permute-start) | collective-permute-done | bytes 262176 | tf_op jit(solution)/shard_map/ppermute | solution.py:303
  274.8 0.8 pad_maximum_fusion
  275.7 0.0 all-gather.4.cloned.1.call-update
  275.7 0.0 copy-done.3
  275.7 0.1 select_reduce_fusion
  275.8 0.2 copy.15
  276.0 47.0 %all-gather.4.cloned.1.call-done.k_ref.v_ref = bf16[2048,1024]{1,0:T(8,128)(2,1)} async-done(((bf16[256,1024]{1,0:T(8,128)(2,1)}), bf16[2048,1024]{1,0:T(8,128)(2,1)}) %all-gather.4.cloned.1.call-update) | async-done | bytes 4194320 | tf_op jit(solution)/shard_map/all_gather | solution.py:305
  323.0 0.0 copy-start
  323.0 2.2 copy-done
  325.2 62.7 %shard_map.78 = (bf16[256,8192]{1,0:T(8,128)(2,1)}, f32[256,64]{1,0:T(8,128)S(1)}) custom-call(f32[256,1]{1,0:T(8,128)S(1)} %convert_element_type.32.live_ref, bf16[256,8192]{1,0:T(8,128)(2,1)S(1)} %copy-done, bf16[2048,1024]{1,0:T(8,128)(2,1)} %all-gather.4.cloned.1.call-done.k_ref.v_ref, bf16[2048,1024]{1,0:T(8,128)(2,1)} %all-gather.4.cloned.1.call-done.k_ref.v_ref), custom_call_target="tpu_custom_call" | custom-call | tf_op jit(solution)/shard_map/pallas_call | solution.py:68
  387.9 0.7 copy.16
  (13 shorter events, 0.2 us)
Async XLA Ops:
  7.2 258.9 %reduce-scatter.2.cloned.1.call-start = ((), (), s32[]{:S(2)}) async-start(), calls=%async_computation.1 | async-start | bytes 9437184 | tf_op jit(solution)/shard_map/reduce_scatter | solution.py:291
  33.5 118.5 %copy-start.2 = (bf16[2048,512]{1,0:T(8,128)(2,1)S(1)}, bf16[2048,512]{1,0:T(8,128)(2,1)}, u32[]{:S(2)}) copy-start(bf16[2048,512]{1,0:T(8,128)(2,1)} %kw_ref.1) | copy-start | bytes 6291460
  33.5 118.5 %dynamic-slice-start = ((f32[16384]{0:T(1024)}, s32[]{:T(128)}), f32[2048]{0:T(1024)S(1)}, s32[]{:S(2)}) async-start(f32[16384]{0:T(1024)} %param.9, s32[]{:T(128)} %select_n.38), calls=%async_computation.3 | async-start | bytes 16896 | tf_op jit(solution)/shard_map/dynamic_slice | solution.py:287
  166.9 156.1 %all-gather.4.cloned.1.call-start = ((), (), s32[]{:S(2)}) async-start(), calls=%async_computation.2 | async-start | bytes 4718592 | tf_op jit(solution)/shard_map/all_gather | solution.py:305
  266.0 2.2 copy-start.1
  267.2 8.5 %copy-start.3 = (s32[4]{0:T(128)S(1)}, s32[4]{0:T(128)}, u32[]{:S(2)}) copy-start(s32[4]{0:T(128)} %param.7) | copy-start | bytes 52
  268.4 6.4 %collective-permute-start = (bf16[128,1024]{1,0:T(8,128)(2,1)S(1)}, bf16[128,1024]{1,0:T(8,128)(2,1)S(1)}, u32[]{:S(2)}, u32[]{:S(2)}) collective-permute-start(bf16[128,1024]{1,0:T(8,128)(2,1)S(1)} %pad_maximum_fusion.1), channel_id=1, source_target_pairs={{0,2},{2,0},{1,3},{3,1},{4,6},{6,4},{5,7},{7,5},{8,10},{10,8},{9,1... | collective-permute-start | bytes 786440 | tf_op jit(solution)/shard_map/ppermute | solution.py:303
  323.0 2.2 copy-start
Sparse Core Ops, SparseCore 0:
  167.0 98.9 reduce-scatter.1
  275.8 47.1 all-gather.3

commit v2 on v1

--- a/solution.py
+++ b/solution.py
@@ -63,7 +63,7 @@
     prompt = keys.shape[0]
     q_heads = width // HD
     group = q_heads // kv_heads
-    heads = 4
+    heads = 8 if group % 8 == 0 else 4
     live = row_live.astype(jnp.float32)[:, None]
     return pl.pallas_call(
         functools.partial(attend_kernel, heads, group),
@@ -110,8 +110,9 @@
 
 
 def move_kernel(
-    x_ref, kw_ref, vw_ref, xin, kwo, vwo, relay,
+    x_ref, kw_ref, vw_ref, sq_ref, xin, kwo, vwo, sqo, relay,
     relay_send, relay_recv, x_send, x_recv, x_local, w_send, w_recv, f_send, f_recv,
+    sq_send, sq_recv, sq_local,
 ):
     groups, fsdp, mp, sub = (lax.axis_index(a) for a in ("groups", "fsdp", "mp", "sub"))
     depth = lax.axis_size("fsdp")
@@ -134,21 +135,53 @@
         return parts - 1 - n
 
     half = kw_ref.shape[0] // 2
-    near = pl.ds(pl.multiple_of(groups * half, half), half)
-
-    def weight_copy(i, src, dst):
+    pieces = 4
+    piece = half // pieces
+    weights = ((kw_ref, kwo), (vw_ref, vwo))
+
+    def piece_rows(owner, p):
+        return pl.ds(pl.multiple_of(owner * half + p * piece, piece), piece)
+
+    def weight_copy(n):
+        src, dst = weights[n // pieces]
+        near = piece_rows(groups, n % pieces)
         return pltpu.make_async_remote_copy(
             src_ref=src.at[near, :], dst_ref=dst.at[near, :],
-            send_sem=w_send.at[i], recv_sem=w_recv.at[i],
+            send_sem=w_send.at[n], recv_sem=w_recv.at[n],
             device_id=(groups, fsdp, 1 - mp, sub), device_id_type=MESH,
         )
 
-    def weight_forward(i, dst):
+    def weight_forward(n, owner):
+        dst = weights[n // pieces][1]
+        near = piece_rows(owner, n % pieces)
         return pltpu.make_async_remote_copy(
             src_ref=dst.at[near, :], dst_ref=dst.at[near, :],
-            send_sem=f_send.at[i], recv_sem=f_recv.at[i],
+            send_sem=f_send.at[n], recv_sem=f_recv.at[n],
             device_id=(1 - groups, fsdp, mp, sub), device_id_type=MESH,
         )
+
+    def pass_weight(n):
+        weight_copy(n).wait_recv()
+        weight_forward(n, groups).start()
+
+    def square_copy(n):
+        return pltpu.make_async_remote_copy(
+            src_ref=sq_ref, dst_ref=sqo.at[mp, fsdp],
+            send_sem=sq_send.at[n], recv_sem=sq_recv.at[mp, fsdp],
+            device_id=(groups, n // 2, sub, n % 2), device_id_type=MESH,
+        )
+
+    def square_here(n):
+        return jnp.logical_and(mine, jnp.logical_and(fsdp == n // 2, sub == n % 2))
+
+    for n in range(2 * depth):
+        @pl.when(square_here(n))
+        def _():
+            pltpu.make_async_copy(sq_ref, sqo.at[mp, fsdp], sq_local).start()
+
+        @pl.when(jnp.logical_not(square_here(n)))
+        def _():
+            square_copy(n).start()
 
     def target(j):
         return (depth // 2) * sub + j // 2, j % 2
@@ -184,32 +217,30 @@
         def _():
             chunk_copy(j, src).wait_send()
 
-    weights = ((kw_ref, kwo), (vw_ref, vwo))
+    after = ((), (0, 1), (2, 3), (4, 5, 6, 7))
 
     @pl.when(jnp.logical_not(mine))
     def _():
         for n in range(parts):
             relay_copy(order(n)).start()
+            for i in after[n]:
+                weight_copy(i).start()
+        for n in range(parts):
+            j = order(n)
+            relay_copy(j).wait_recv()
+            send_chunk(j, relay.at[j])
+            for i in after[n]:
+                pass_weight(i)
 
     @pl.when(mine)
     def _():
         for n in range(parts):
             j = order(n)
             send_chunk(j, x_ref.at[:, pl.ds(j * width, width)])
-
-    for i, (src, dst) in enumerate(weights):
-        weight_copy(i, src, dst).start()
-
-    @pl.when(jnp.logical_not(mine))
-    def _():
-        for n in range(parts):
-            j = order(n)
-            relay_copy(j).wait_recv()
-            send_chunk(j, relay.at[j])
-
-    for i, (src, dst) in enumerate(weights):
-        weight_copy(i, src, dst).wait_recv()
-        weight_forward(i, dst).start()
+        for i in range(2 * pieces):
+            weight_copy(i).start()
+        for i in range(2 * pieces):
+            pass_weight(i)
 
     @pl.when(mine)
     def _():
@@ -234,18 +265,34 @@
                 device_id=(groups, z, mp, fsdp // (depth // 2)), device_id_type=MESH,
             ).wait_recv()
 
-    far = pl.ds(pl.multiple_of((1 - groups) * half, half), half)
-    for i, (src, dst) in enumerate(weights):
-        weight_copy(i, src, dst).wait_send()
-        weight_forward(i, dst).wait_send()
-        pltpu.make_async_remote_copy(
-            src_ref=dst.at[far, :], dst_ref=dst.at[far, :],
-            send_sem=f_send.at[i], recv_sem=f_recv.at[i],
-            device_id=(1 - groups, fsdp, mp, sub), device_id_type=MESH,
-        ).wait_recv()
-
-
-def move(prompt_x, key_weight, value_weight):
+    for n in range(2 * pieces):
+        weight_copy(n).wait_send()
+        weight_forward(n, groups).wait_send()
+        weight_forward(n, 1 - groups).wait_recv()
+
+    for n in range(2 * depth):
+        @pl.when(square_here(n))
+        def _():
+            pltpu.make_async_copy(sq_ref, sqo.at[mp, fsdp], sq_local).wait()
+
+        @pl.when(jnp.logical_not(square_here(n)))
+        def _():
+            square_copy(n).wait_send()
+
+    for m in range(2):
+        for z in range(depth):
+            here = jnp.logical_and(mine, jnp.logical_and(mp == m, fsdp == z))
+
+            @pl.when(jnp.logical_not(here))
+            def _():
+                pltpu.make_async_remote_copy(
+                    src_ref=sqo.at[m, z], dst_ref=sqo.at[m, z],
+                    send_sem=sq_send.at[0], recv_sem=sq_recv.at[m, z],
+                    device_id=(groups, z, m, mp), device_id_type=MESH,
+                ).wait_recv()
+
+
+def move(prompt_x, key_weight, value_weight, squares):
     depth = lax.axis_size("fsdp")
     rows = prompt_x.shape[0]
     width = key_weight.shape[0]
@@ -258,16 +305,17 @@
             jax.ShapeDtypeStruct((depth, rows, width), jnp.bfloat16),
             jax.ShapeDtypeStruct(key_weight.shape, jnp.bfloat16),
             jax.ShapeDtypeStruct(value_weight.shape, jnp.bfloat16),
+            jax.ShapeDtypeStruct((2, depth) + squares.shape, jnp.float32),
             jax.ShapeDtypeStruct((parts, rows, width), jnp.bfloat16),
         ),
-        in_specs=[anywhere] * 3,
-        out_specs=(anywhere,) * 4,
+        in_specs=[anywhere] * 4,
+        out_specs=(anywhere,) * 5,
         scratch_shapes=[
             dma((parts,)), dma((parts,)), dma((parts,)), dma((depth,)), dma(()),
-            dma((2,)), dma((2,)), dma((2,)), dma((2,)),
+            dma((8,)), dma((8,)), dma((8,)), dma((8,)), dma((2 * depth,)), dma((2, depth)), dma(()),
         ],
         compiler_params=pltpu.CompilerParams(collective_id=0, has_side_effects=True),
-    )(prompt_x, key_weight, value_weight)
+    )(prompt_x, key_weight, value_weight, squares)
 
 
 def body_split(queries, lengths, prompt_x, norm_gain, key_weight, value_weight):
@@ -279,11 +327,10 @@
     kv_heads = kv_width // HD
     widened = prompt_x.astype(jnp.float32)
     squares = jnp.sum(widened * widened, axis=1)
-    squares = lax.all_gather(squares, ("mp", "fsdp", "sub"), axis=0, tiled=False)
-    squares = squares.reshape(2, depth, 2, prompt_rows).sum(axis=0)
-    squares = lax.dynamic_index_in_dim(squares, mp, axis=1, keepdims=False).reshape(depth * prompt_rows)
+    squares = jnp.broadcast_to(squares[None, :], (8, prompt_rows))
+    gathered, other_key, other_value, squares, _ = move(prompt_x, key_weight, value_weight, squares)
+    squares = squares[:, :, 0, :].sum(axis=0).reshape(depth * prompt_rows)
     scale = lax.rsqrt(squares / norm_gain.shape[0] + norm_eps)
-    gathered, other_key, other_value, _ = move(prompt_x, key_weight, value_weight)
     gain = lax.dynamic_slice_in_dim(norm_gain, my_index * features, features)
     gathered = gathered.reshape(depth * prompt_rows, features).astype(jnp.float32)
     normed = (gathered * scale[:, None] * gain[None, :]).astype(jnp.bfloat16)

time: 396 us -> 383 us (0.967)
  blocking collectives: 23.1 us -> 0 us
  waiting for transfers between devices: 150 us -> 167 us
  Pallas kernels: 181 us -> 173 us
    all_gather x1 -> x0, blocking collectives: 23.1 us -> none  [body_split(): lax.all_gather(squares, ('mp', 'fsdp', 'sub'), axis=0, tiled=False)]
    reduce_scatter x1, waiting for transfers between devices: 98.6 us -> 116 us  [body_split(): lax.psum_scatter(jnp.dot(normed, weights, preferred_element_type=jnp.floa...]
    pallas_call x1, Pallas kernels: 118 us -> 113 us  [move(): pl.pallas_call(move_kernel, out_shape=(jax.ShapeDtypeStruct((depth, rows,...]
where the time goes in v2:
time: 383 us
  Pallas kernels  173 us (45%)
  waiting for transfers between devices  167 us (44%)
  matrix products  14.9 us (4%)
  between operations  14.2 us (4%)
  other arithmetic  6.17 us (2%)
  local copies, waits for them, and re-layouts  5.8 us (2%)
    reduce_scatter x1, waiting for transfers between devices, body_split(): lax.psum_scatter(jnp.dot(normed, weights, preferred_element_type=jnp.floa...  116 us
    pallas_call x1, Pallas kernels, move(): pl.pallas_call(move_kernel, out_shape=(jax.ShapeDtypeStruct((depth, rows,...  113 us
    pallas_call x1, Pallas kernels, attend(): pl.pallas_call(functools.partial(attend_kernel, heads, group), grid=(q_he...  60 us
    all_gather x1, waiting for transfers between devices, body_split(): cache = lax.all_gather(both, ('fsdp', 'sub'), axis=0, tiled=True)  47 us
    dot_general x1, matrix products, body_split(): jnp.dot(normed, weights, preferred_element_type=jnp.float32)  14.9 us
  transfers between devices with their start and end apart: 3, of which 3 were waited for; matrix products, arithmetic and copies ran while one was open for 0% of the time, Pallas kernels for 0%

profile of v2, /device:TPU:0, one launch (start us, length us, event | category | flops | bytes accessed | tf_op | source)
XLA Modules:
  0.0 383.1 jit_solution(9622026918131504213)
XLA Ops:
  7.2 0.0 reduce-scatter.2.cloned.1.call-start
  7.2 3.1 multiply_reduce_fusion
  10.3 0.6 broadcast_in_dim.12.sq_ref
  10.9 0.0 copy-start.2
  10.9 112.8 %shard_map.77 = (bf16[4,256,2048]{2,1,0:T(8,128)(2,1)}, bf16[2048,512]{1,0:T(8,128)(2,1)}, bf16[2048,512]{1,0:T(8,128)(2,1)}, f32[2,4,8,256]{3,2,1,0:T(8,128)}, bf16[4,256,2048]{2,1,0:T(8,128)(2,1)}) custom-call(bf16[256,8192]{1,0:T(8,128)(2,1)} %x_ref.1, bf16[2048,512]{1,0:T(8,128)(2,1)} %kw_ref.1, bf16[2048,512]{1,0:T(8,128)(2,1)} %vw_ref.1, ...), custom_call_target="tpu_custom_call" | custom-call | tf_op jit(solution)/shard_map/pallas_call | solution.py:302
  123.7 0.9 slice_reduce_fusion
  124.6 0.7 dynamic_slice.3
  125.3 0.0 copy-done.2
  125.3 14.9 %fusion = f32[1024,2048]{1,0:T(8,128)} fusion(bf16[2048,512]{1,0:T(8,128)(2,1)} %get-tuple-element.9, bf16[2048,512]{1,0:T(8,128)(2,1)} %get-tuple-element.8, bf16[2048,512]{1,0:T(8,128)(2,1)} %vw_ref.1, bf16[2048,512]{1,0:T(8,128)(2,1)S(1)} %copy-done.2, bf16[1024,2048]{1,0:T(8,128)(2,1)} %bitcast.20, f32[2048]{0:T(1024)S(1)} %dynamic_slice.3, ...), kind=kOutput, calls=%fused_computation | convolution fusion | flops 8631877632 | bytes 20983808 | tf_op jit(solution)/shard_map/dot_general | solution.py:339
  140.3 0.0 reduce-scatter.2.cloned.1.call-update
  140.3 0.2 all-gather.2.cloned.1.call-start
  140.6 0.3 multiply_cosine_fusion
  140.9 115.5 %reduce-scatter.2.cloned.1.call-done = f32[128,2048]{1,0:T(8,128)} async-done(((f32[1024,2048]{1,0:T(8,128)}), f32[128,2048]{1,0:T(8,128)}) %reduce-scatter.2.cloned.1.call-update) | async-done | bytes 1048592 | tf_op jit(solution)/shard_map/reduce_scatter | solution.py:338
  256.4 0.0 copy-start.1
  256.4 1.2 fusion.16
  257.5 0.0 copy-start.3
  257.5 0.1 reshape.163
  257.6 0.1 reshape.165
  257.7 0.5 subtract_convert_fusion.1
  258.2 0.4 pad_maximum_fusion.2
  258.6 0.0 copy-done.1
  258.6 0.1 convert.25
  258.7 1.5 collective-permute-start
  260.3 4.9 %collective-permute-done = bf16[128,1024]{1,0:T(8,128)(2,1)S(1)} collective-permute-done((bf16[128,1024]{1,0:T(8,128)(2,1)S(1)}, bf16[128,1024]{1,0:T(8,128)(2,1)S(1)}, u32[]{:S(2)}, u32[]{:S(2)}) %collective-permute-start) | collective-permute-done | bytes 262176 | tf_op jit(solution)/shard_map/ppermute | solution.py:350
  265.2 0.8 pad_maximum_fusion
  266.0 0.0 all-gather.2.cloned.1.call-update
  266.1 0.0 copy-done.3
  266.1 0.1 select_reduce_fusion
  266.2 0.2 copy.13
  266.4 47.0 %all-gather.2.cloned.1.call-done.k_ref.v_ref = bf16[2048,1024]{1,0:T(8,128)(2,1)} async-done(((bf16[256,1024]{1,0:T(8,128)(2,1)}), bf16[2048,1024]{1,0:T(8,128)(2,1)}) %all-gather.2.cloned.1.call-update) | async-done | bytes 4194320 | tf_op jit(solution)/shard_map/all_gather | solution.py:352
  313.4 0.0 copy-start
  313.4 2.2 copy-done
  315.6 60.0 %shard_map.78 = (bf16[256,8192]{1,0:T(8,128)(2,1)}, f32[256,64]{1,0:T(8,128)S(1)}) custom-call(f32[256,1]{1,0:T(8,128)S(1)} %convert_element_type.32.live_ref, bf16[256,8192]{1,0:T(8,128)(2,1)S(1)} %copy-done, bf16[2048,1024]{1,0:T(8,128)(2,1)} %all-gather.2.cloned.1.call-done.k_ref.v_ref, bf16[2048,1024]{1,0:T(8,128)(2,1)} %all-gather.2.cloned.1.call-done.k_ref.v_ref), custom_call_target="tpu_custom_call" | custom-call | tf_op jit(solution)/shard_map/pallas_call | solution.py:68
  375.6 0.7 copy.14
  (11 shorter events, 0.2 us)
Async XLA Ops:
  7.2 249.2 %reduce-scatter.2.cloned.1.call-start = ((), (), s32[]{:S(2)}) async-start(), calls=%async_computation.1 | async-start | bytes 9437184 | tf_op jit(solution)/shard_map/reduce_scatter | solution.py:338
  10.9 114.4 %copy-start.2 = (bf16[2048,512]{1,0:T(8,128)(2,1)S(1)}, bf16[2048,512]{1,0:T(8,128)(2,1)}, u32[]{:S(2)}) copy-start(bf16[2048,512]{1,0:T(8,128)(2,1)} %kw_ref.1) | copy-start | bytes 6291460
  140.3 173.1 %all-gather.2.cloned.1.call-start = ((), (), s32[]{:S(2)}) async-start(), calls=%async_computation.2 | async-start | bytes 4718592 | tf_op jit(solution)/shard_map/all_gather | solution.py:352
  256.4 2.2 copy-start.1
  257.5 8.5 %copy-start.3 = (s32[4]{0:T(128)S(1)}, s32[4]{0:T(128)}, u32[]{:S(2)}) copy-start(s32[4]{0:T(128)} %param.7) | copy-start | bytes 52
  258.7 6.4 %collective-permute-start = (bf16[128,1024]{1,0:T(8,128)(2,1)S(1)}, bf16[128,1024]{1,0:T(8,128)(2,1)S(1)}, u32[]{:S(2)}, u32[]{:S(2)}) collective-permute-start(bf16[128,1024]{1,0:T(8,128)(2,1)S(1)} %pad_maximum_fusion.1), channel_id=1, source_target_pairs={{0,2},{2,0},{1,3},{3,1},{4,6},{6,4},{5,7},{7,5},{8,10},{10,8},{9,1... | collective-permute-start | bytes 786440 | tf_op jit(solution)/shard_map/ppermute | solution.py:350
  313.4 2.2 copy-start
Sparse Core Ops, SparseCore 0:
  140.4 115.9 reduce-scatter.1
  266.2 47.1 all-gather.1
